TPU v7x, 512 devices: a whole 4x4x16 slice. The times are simulated.
512 devices in a mesh: attn: 4 (over x), tp: 8 (over y, core), exp: 16 (over z).
Axes of the slice: x: 4, y: 4, z: 16, core: 2. Of those that a mesh axis runs over, the one named last changes fastest.
Arguments:
- queries: bfloat16 [64, 6144], P(('attn', 'exp'), 'tp'), may hold values from -6 to 6
- cache_keys: bfloat16 [64, 512, 1024], P(('attn', 'exp'), None, 'tp'), may hold values from -6 to 6
- cache_values: bfloat16 [64, 512, 1024], P(('attn', 'exp'), None, 'tp'), may hold values from -6 to 6
- new_keys: bfloat16 [64, 1024], P(('attn', 'exp'), 'tp'), may hold values from -6 to 6
- new_values: bfloat16 [64, 1024], P(('attn', 'exp'), 'tp'), may hold values from -6 to 6
- lengths: int32 [64], P(('attn', 'exp')), may hold values from 1 to 512, 16384 in all
- moe_input: bfloat16 [1024, 3072], P(('attn', 'exp'), 'tp'), may hold values from -6 to 6
- router_weight: bfloat16 [8, 3072], P(None, 'tp'), may hold values from -0.109375 to 0.109375
- expert_ids: int32 [1024, 2], P(('attn', 'exp')), may hold values from 0 to 7, all different within a row; in each aligned block of 16 rows (0 to 15, 16 to 31, ...) at most 5 rows name the same one
- gate_weight: bfloat16 [16, 3072, 8192], P('exp', None, ('attn', 'tp')), may hold values from -0.109375 to 0.109375
- up_weight: bfloat16 [16, 3072, 8192], P('exp', None, ('attn', 'tp')), may hold values from -0.109375 to 0.109375
- down_weight: bfloat16 [16, 8192, 3072], P('exp', ('attn', 'tp')), may hold values from -0.09375 to 0.09375
Outputs:
- attention_out: bfloat16 [64, 6144], P(('attn', 'exp'), 'tp')
- expert_out: bfloat16 [1024, 3072], P(('attn', 'exp'), 'tp')
Inputs may be any that keep to these rules, and one draw needn't show every extreme that they name: `expert_ids`: each row names two different experts. Among the rows of one device (aligned blocks of 16 rows) no expert is named more than 5 times, and some block names one expert exactly 5 times. `lengths`: some row has exactly 512 cached positions.
All inputs are finite; a program needn't handle non-finite values. No bound on the sum of `lengths` on one device may be relied on, other than what follows from the above.
Results may differ from a plain program's by a relative error of at most 0.02.
Values may be sent and summed in bfloat16 or wider, within the bound.
A program may use at most 64 MiB of HBM per device.

v0:
```python
import math

import jax
import jax.numpy as jnp
from jax import lax
from jax.sharding import PartitionSpec as P

HD = 128
CAP = 5


def attend(queries, cache_keys, cache_values, new_keys, new_values, lengths):
    row_count = queries.shape[0]
    positions = cache_keys.shape[1]
    kv_local = cache_keys.shape[2] // HD
    per_key = queries.shape[1] // cache_keys.shape[2]
    score_scale = 1.0 / math.sqrt(HD)
    query_heads = queries.reshape(row_count, kv_local, per_key, HD)
    key_heads = cache_keys.reshape(row_count, positions, kv_local, HD)
    value_heads = cache_values.reshape(row_count, positions, kv_local, HD)
    own_keys = new_keys.reshape(row_count, kv_local, HD)
    own_values = new_values.reshape(row_count, kv_local, HD)
    scores = (
        jnp.einsum("rhgd,rphd->rhgp", query_heads, key_heads, preferred_element_type=jnp.float32)
        * score_scale
    )
    own_score = (
        jnp.einsum("rhgd,rhd->rhg", query_heads, own_keys, preferred_element_type=jnp.float32)
        * score_scale
    )
    visible = jnp.arange(positions, dtype=jnp.int32)[None, :] < lengths[:, None]
    scores = jnp.where(visible[:, None, None, :], scores, -jnp.inf)
    peak = jnp.maximum(jnp.max(scores, axis=-1), own_score)
    weights = jnp.exp(scores - peak[..., None])
    own_weight = jnp.exp(own_score - peak)
    total = jnp.sum(weights, axis=-1) + own_weight
    weights_bf = (weights / total[..., None]).astype(jnp.bfloat16)
    own_bf = (own_weight / total).astype(jnp.bfloat16)
    result = jnp.einsum(
        "rhgp,rphd->rhgd", weights_bf, value_heads, preferred_element_type=jnp.float32
    )
    result = (
        result
        + own_bf.astype(jnp.float32)[..., None] * own_values.astype(jnp.float32)[:, :, None, :]
    )
    return result.reshape(row_count, -1).astype(jnp.bfloat16)


def slot_numbers(expert_ids, experts):
    flat_ids = expert_ids.reshape(-1)
    onehot = (flat_ids[:, None] == jnp.arange(experts, dtype=jnp.int32)[None, :]).astype(jnp.int32)
    before = jnp.cumsum(onehot, axis=0) - onehot
    return jnp.sum(before * onehot, axis=1).reshape(expert_ids.shape)


def pack_rows(row_tile_block, id_block, experts, capacity):
    slot_ids = slot_numbers(id_block, experts)
    target = (id_block * capacity + slot_ids).reshape(-1)
    placement = (
        jnp.arange(experts * capacity, dtype=jnp.int32)[:, None] == target[None, :]
    ).astype(row_tile_block.dtype)
    doubled = jnp.repeat(row_tile_block, 2, axis=0)
    packed = jnp.dot(placement, doubled, preferred_element_type=jnp.float32).astype(
        row_tile_block.dtype
    )
    feature_count = row_tile_block.shape[1]
    packed = packed.reshape(experts, 1, capacity, feature_count)
    packed = jnp.broadcast_to(packed, (experts, 2, capacity, feature_count))
    return packed.reshape(2 * experts, capacity, feature_count)


def body(
    queries,
    cache_keys,
    cache_values,
    new_keys,
    new_values,
    lengths,
    moe_input,
    router_weight,
    expert_ids,
    gate_weight,
    up_weight,
    down_weight,
):
    attention_out = attend(queries, cache_keys, cache_values, new_keys, new_values, lengths)
    attn_count = lax.axis_size("attn")
    tp_count = lax.axis_size("tp")
    exp_count = lax.axis_size("exp")
    experts = router_weight.shape[0]
    capacity = CAP
    width = moe_input.shape[1]
    local_halves = gate_weight.shape[0]
    hidden_neuron_count = gate_weight.shape[2]
    sources = exp_count * capacity
    partial_logits = jnp.einsum(
        "rd,ed->re", moe_input, router_weight, preferred_element_type=jnp.float32
    )
    logits = lax.psum(partial_logits, "tp")
    chosen = jnp.take_along_axis(logits, expert_ids, axis=1)
    mixing = jax.nn.sigmoid(chosen - chosen[:, ::-1])
    slot_ids = slot_numbers(expert_ids, experts)
    packed = pack_rows(moe_input, expert_ids, experts, capacity)
    arrived = lax.all_to_all(packed, "exp", split_axis=0, concat_axis=1, tiled=True)
    initial = jnp.zeros((local_halves, attn_count * sources, hidden_neuron_count), jnp.float32)
    piece = lax.all_gather(arrived[None], ("attn", "tp"), axis=0, tiled=True)

    def add_one(step_index, running):
        row_group = step_index // tp_count
        feature_part = step_index % tp_count
        token_tile_block = lax.dynamic_index_in_dim(piece, step_index, 0, keepdims=False)
        gate_matrix_rows = lax.dynamic_slice_in_dim(gate_weight, feature_part * width, width, 1)
        up_projection_rows = lax.dynamic_slice_in_dim(up_weight, feature_part * width, width, 1)
        gate_add = jnp.einsum(
            "qou,quh->qoh", token_tile_block, gate_matrix_rows, preferred_element_type=jnp.float32
        )
        up_add = jnp.einsum(
            "qou,quh->qoh", token_tile_block, up_projection_rows, preferred_element_type=jnp.float32
        )
        offset = row_group * sources
        gate_now = lax.dynamic_slice_in_dim(running[0], offset, sources, 1) + gate_add
        up_now = lax.dynamic_slice_in_dim(running[1], offset, sources, 1) + up_add
        gate_next = lax.dynamic_update_slice_in_dim(running[0], gate_now, offset, 1)
        up_next = lax.dynamic_update_slice_in_dim(running[1], up_now, offset, 1)
        return (gate_next, up_next)

    gate_sum, up_sum = lax.fori_loop(0, piece.shape[0], add_one, (initial, initial))
    hidden_act = (jax.nn.silu(gate_sum) * up_sum).astype(jnp.bfloat16)

    def one_term(piece_index):
        row_group = piece_index // tp_count
        feature_part = piece_index % tp_count
        row_tile_block = lax.dynamic_slice_in_dim(hidden_act, row_group * sources, sources, 1)
        down_projection_columns = lax.dynamic_slice_in_dim(
            down_weight, feature_part * width, width, 2
        )
        return jnp.einsum(
            "pml,plg->pmg",
            row_tile_block,
            down_projection_columns,
            preferred_element_type=jnp.float32,
        )

    summed = lax.psum_scatter(
        lax.map(one_term, jnp.arange(1 * lax.axis_size(("attn", "tp")), dtype=jnp.int32)).astype(
            jnp.bfloat16
        ),
        ("attn", "tp"),
        scatter_dimension=0,
        tiled=True,
    ).astype(jnp.float32)
    returned = lax.all_to_all(
        summed[0].astype(jnp.bfloat16), "exp", split_axis=1, concat_axis=0, tiled=True
    ).astype(jnp.float32)
    pair_sum = jnp.sum(returned.reshape(experts, 2, capacity, width), axis=1)
    selected_experts = pair_sum.reshape(experts * capacity, width)[expert_ids * capacity + slot_ids]
    expert_out = jnp.sum(mixing[..., None] * selected_experts, axis=1).astype(jnp.bfloat16)
    return (attention_out, expert_out)


def solution(mesh):
    placed = (
        P(("attn", "exp"), "tp"),
        P(("attn", "exp"), None, "tp"),
        P(("attn", "exp"), None, "tp"),
        P(("attn", "exp"), "tp"),
        P(("attn", "exp"), "tp"),
        P(("attn", "exp")),
        P(("attn", "exp"), "tp"),
        P(None, "tp"),
        P(("attn", "exp"), None),
        P("exp", None, ("attn", "tp")),
        P("exp", None, ("attn", "tp")),
        P("exp", ("attn", "tp"), None),
    )
    return jax.shard_map(
        body,
        mesh=mesh,
        in_specs=placed,
        out_specs=(P(("attn", "exp"), "tp"), P(("attn", "exp"), "tp")),
        check_vma=False,
    )
```

profile of v0, /device:TPU:1, one launch (start us, length us, event | category | flops | bytes accessed | tf_op | source)
XLA Modules:
  0.0 458.9 jit_solution(4271097207558733577)
XLA Ops:
  10.4 27.4 %all_to_all.8 = bf16[16,5,384]{2,1,0:T(8,128)(2,1)S(1)} all-to-all(bf16[16,5,384]{2,1,0:T(8,128)(2,1)S(1)} %bitcast.107), channel_id=1, replica_groups=mesh['attn'=4,'tp'=8,'exp'=16] {'exp'}, dimensions={0} | all-to-all | bytes 122880 | tf_op jit(solution)/shard_map/all_to_all | solution.py:104
  38.5 54.3 %all-gather.2.cloned.1.call-done = bf16[32,1,80,384]{3,2,1,0:T(8,128)(2,1)} async-done(((bf16[1,1,80,384]{3,2,1,0:T(8,128)(2,1)}), bf16[32,1,80,384]{3,2,1,0:T(8,128)(2,1)}) %all-gather.2.cloned.1.call-update) | async-done | bytes 1966096 | tf_op jit(solution)/shard_map/all_gather | solution.py:106
  92.9 74.6 %while.29 = (s32[]{:T(128)}, f32[1,320,256]{2,1,0:T(8,128)S(1)}, f32[1,320,256]{2,1,0:T(8,128)S(1)}, bf16[32,1,80,384]{3,2,1,0:T(8,128)(2,1)}, bf16[1,3072,256]{...) while((s32[]{:T(128)}, f32[1,320,256]{2,1,0:T(8,128)S(1)}, ...), condition=%wide.region_6.7_spmd, body=%wide.region_5.6_spmd.sunk | while | flops 31498260 | bytes 845172 | solution.py:127
  112.7 1.1 fusion.54
  115.1 1.1 fusion.54
  117.4 1.1 fusion.54
  119.7 1.1 fusion.54
  122.1 1.1 fusion.54
  124.4 1.1 fusion.54
  126.7 1.1 fusion.54
  129.1 1.1 fusion.54
  167.7 157.9 %while.30 = (s32[]{:T(128)}, bf16[32,1,80,384]{3,2,1,0:T(8,128)(2,1)}, s32[32]{0:T(128)S(1)}, bf16[1,320,256]{2,1,0:T(8,128)(2,1)S(1)}, bf16[1,256,3072]{2,1,0:T...) while((s32[]{:T(128)}, ...), condition=%wide.region_8.9_spmd, body=%wide.region_7.8_spmd.sunk | while | flops 15728669 | bytes 361400 | solution.py:145
  170.9 1.7 fusion.58
  175.9 1.7 fusion.58
  180.8 1.7 fusion.58
  185.7 1.7 fusion.58
  190.7 1.7 fusion.58
  195.6 1.7 fusion.58
  200.5 1.7 fusion.58
  205.5 1.7 fusion.58
  210.4 1.7 fusion.58
  215.3 1.7 fusion.58
  220.3 1.7 fusion.58
  225.2 1.7 fusion.58
  230.1 1.7 fusion.58
  235.1 1.7 fusion.58
  240.0 1.7 fusion.58
  245.0 1.7 fusion.58
  249.9 1.7 fusion.58
  254.8 1.7 fusion.58
  259.8 1.7 fusion.58
  264.7 1.7 fusion.58
  269.6 1.7 fusion.58
  274.6 1.7 fusion.58
  279.5 1.7 fusion.58
  284.4 1.7 fusion.58
  289.4 1.7 fusion.58
  294.3 1.7 fusion.58
  299.2 1.7 fusion.58
  304.1 1.7 fusion.58
  309.1 1.7 fusion.58
  314.0 1.7 fusion.58
  318.9 1.7 fusion.58
  323.9 1.7 fusion.58
  328.2 12.0 %psum.7 = f32[16,8]{0,1:T(8,128)S(1)} all-reduce(f32[16,8]{0,1:T(8,128)S(1)} %fusion.37), channel_id=1, replica_groups=mesh['attn'=4,'tp'=8,'exp'=16] {'tp'}, use_global_device_ids=true, to_apply=%region_2.3 | all-reduce | flops 128 | bytes 1024 | tf_op jit(solution)/shard_map/psum | solution.py:99
  341.1 82.3 %reduce-scatter.2.cloned.1.call-done = bf16[1,1,80,384]{3,2,1,0:T(8,128)(2,1)} async-done(((bf16[32,1,80,384]{3,2,1,0:T(8,128)(2,1)}), bf16[1,1,80,384]{3,2,1,0:T(8,128)(2,1)}) %reduce-scatter.2.cloned.1.call-update) | async-done | bytes 61456 | tf_op jit(solution)/shard_map/reduce_scatter | solution.py:144
  426.6 12.0 %all-to-all-start.1 = ((bf16[16,2,960]{2,1,0:T(2,128)(2,1)}), bf16[16,2,960]{2,1,0:T(2,128)(2,1)S(1)}, u32[]{:S(2)}, u32[]{:S(2)}) async-start(bf16[16,2,960]{2,1,0:T(2,128)(2,1)} %reshape.247), calls=%async_computation.2 | async-start | bytes 131072 | tf_op jit(solution)/shard_map/all_to_all | solution.py:152
  438.7 11.5 %all-to-all-done.1 = bf16[16,2,960]{2,1,0:T(2,128)(2,1)S(1)} async-done(((bf16[16,2,960]{2,1,0:T(2,128)(2,1)}), bf16[16,2,960]{2,1,0:T(2,128)(2,1)S(1)}, u32[]{:S(2)}, u32[]{:S(2)}) %all-to-all-start.1) | async-done | bytes 61472 | tf_op jit(solution)/shard_map/all_to_all | solution.py:152
  (164 shorter events, 94.5 us)
Async XLA Ops:
  7.2 319.2 %copy-start = (bf16[1,512,128]{2,1,0:T(8,128)(2,1)S(1)}, bf16[1,512,128]{2,1,0:T(8,128)(2,1)}, u32[]{:S(2)}) copy-start(bf16[1,512,128]{2,1,0:T(8,128)(2,1)} %param.17) | copy-start | bytes 393220
  7.2 85.7 %all-gather.2.cloned.1.call-start = ((), (), s32[]{:S(2)}) async-start(), calls=%async_computation.3 | async-start | bytes 2027520 | tf_op jit(solution)/shard_map/all_gather | solution.py:106
  38.5 384.9 %reduce-scatter.2.cloned.1.call-start = ((), (), s32[]{:S(2)}) async-start(), calls=%async_computation.4 | async-start | bytes 2027520 | tf_op jit(solution)/shard_map/reduce_scatter | solution.py:144
  167.6 158.6 %copy-start.4 = (bf16[1,768]{1,0:T(2,128)(2,1)S(1)}, bf16[1,768]{1,0:T(2,128)(2,1)}, u32[]{:S(2)}) copy-start(bf16[1,768]{1,0:T(2,128)(2,1)} %param.16) | copy-start | bytes 4612
  167.6 158.9 %copy-start.6 = (bf16[1,128]{1,0:T(2,128)(2,1)S(1)}, bf16[1,128]{1,0:T(2,128)(2,1)}, u32[]{:S(2)}) copy-start(bf16[1,128]{1,0:T(2,128)(2,1)} %param.19) | copy-start | bytes 772
  167.7 159.3 %copy-start.7 = (bf16[1,128]{1,0:T(2,128)(2,1)S(1)}, bf16[1,128]{1,0:T(2,128)(2,1)}, u32[]{:S(2)}) copy-start(bf16[1,128]{1,0:T(2,128)(2,1)} %param.20) | copy-start | bytes 772
  167.7 159.3 %copy-start.5 = (bf16[1,512,128]{2,1,0:T(8,128)(2,1)S(1)}, bf16[1,512,128]{2,1,0:T(8,128)(2,1)}, u32[]{:S(2)}) copy-start(bf16[1,512,128]{2,1,0:T(8,128)(2,1)} %param.18) | copy-start | bytes 393220
  167.7 160.2 %copy-start.2 = (s32[16,2]{0,1:T(2,128)S(1)}, s32[16,2]{0,1:T(2,128)}, u32[]{:S(2)}) copy-start(s32[16,2]{0,1:T(2,128)} %param.24) | copy-start | bytes 388
  167.7 160.4 %copy-start.1 = (bf16[16,384]{1,0:T(8,128)(2,1)S(1)}, bf16[16,384]{1,0:T(8,128)(2,1)}, u32[]{:S(2)}) copy-start(bf16[16,384]{1,0:T(8,128)(2,1)} %param.22) | copy-start | bytes 36868
  167.7 160.4 %copy-start.3 = (bf16[8,384]{1,0:T(8,128)(2,1)S(1)}, bf16[8,384]{1,0:T(8,128)(2,1)}, u32[]{:S(2)}) copy-start(bf16[8,384]{1,0:T(8,128)(2,1)} %param.23) | copy-start | bytes 18436
  426.6 23.6 %all-to-all-start.1 = ((bf16[16,2,960]{2,1,0:T(2,128)(2,1)}), bf16[16,2,960]{2,1,0:T(2,128)(2,1)S(1)}, u32[]{:S(2)}, u32[]{:S(2)}) async-start(bf16[16,2,960]{2,1,0:T(2,128)(2,1)} %reshape.247), calls=%async_computation.2 | async-start | bytes 131072 | tf_op jit(solution)/shard_map/all_to_all | solution.py:152
Sparse Core Ops, SparseCore 0:
  38.6 54.2 all-gather.1
  325.7 97.6 reduce-scatter.1
where the time goes:
time: 465 us; the launch traced here: 459 us
  waiting for transfers between devices  148 us (32%)
  matrix products  129 us (28%)
  loops' own time  85.5 us (18%)
  blocking collectives  39.4 us (8%)
  local copies, waits for them, and re-layouts  26.2 us (6%)
  between operations  15 us (3%)
  starting transfers between devices  12.1 us (3%)
    another operation x1, loops' own time, body(): lax.map(one_term, jnp.arange(1 * lax.axis_size(('attn', 'tp')), dtype=jnp...  83.9 us
    reduce_scatter x1, waiting for transfers between devices, body(): lax.psum_scatter(lax.map(one_term, jnp.arange(1 * lax.axis_size(('attn',...  82.3 us
    dot_general x32, matrix products, one_term(): jnp.einsum('pml,plg->pmg', row_tile_block, down_projection_columns, prefe...  55.3 us
    all_gather x1, waiting for transfers between devices, body(): piece = lax.all_gather(arrived[None], ('attn', 'tp'), axis=0, tiled=True)  54.3 us
    dot_general x32, matrix products, add_one(): jnp.einsum('qou,quh->qoh', token_tile_block, gate_matrix_rows, preferred_...  36.6 us
    dot_general x32, matrix products, add_one(): jnp.einsum('qou,quh->qoh', token_tile_block, up_projection_rows, preferre...  36.5 us
    all_to_all x1, blocking collectives, body(): lax.all_to_all(packed, 'exp', split_axis=0, concat_axis=1, tiled=True)  27.4 us
    dynamic_slice x32, local copies, waits for them, and re-layouts, body(): lax.map(one_term, jnp.arange(1 * lax.axis_size(('attn', 'tp')), dtype=jnp...  18.6 us
  transfers between devices with their start and end apart: 3, of which 3 were waited for; matrix products, arithmetic and copies ran while one was open for 1% of the time, Pallas kernels for 0%

commit v1 on v0

v1 whole, which is shorter than its diff:
```python
import math

import jax
import jax.numpy as jnp
from jax import lax
from jax.experimental import pallas as pl
from jax.experimental.pallas import tpu as pltpu
from jax.sharding import PartitionSpec as P

MESH = pl.DeviceIdType.MESH
BF = jnp.bfloat16
F32 = jnp.float32
CAP = 5
NX, NY, NZ, NT = 4, 4, 16, 8
W = 384
SLOTROWS = 80
HID = 256
D = 3072


def iota(shape, dim):
    return lax.broadcasted_iota(jnp.int32, shape, dim)


def chunk_of(m):
    return (m >= 5).astype(jnp.int32) + (m >= 10).astype(jnp.int32) + (m >= 15).astype(jnp.int32)


def dot(a, b):
    return jnp.dot(a, b, preferred_element_type=F32)


def drain(ref, sem):
    pltpu.make_async_copy(ref, ref, sem).wait()


def attention(q_ref, ck, cv, nk_ref, nv_ref, len_ref, att_ref):
    scale = 1.0 / math.sqrt(128)
    q = q_ref[...]
    heads = [q[:, h * 128 : (h + 1) * 128] for h in range(6)]
    qh = jnp.concatenate(heads + [jnp.zeros((2, 128), BF)], axis=0)
    scores = lax.dot_general(qh, ck[...], (((1,), (1,)), ((), ())), preferred_element_type=F32) * scale
    own = jnp.sum(qh.astype(F32) * nk_ref[...].astype(F32), axis=1, keepdims=True) * scale
    visible = iota(scores.shape, 1) < len_ref[...]
    scores = jnp.where(visible, scores, -jnp.inf)
    peak = jnp.maximum(jnp.max(scores, axis=1, keepdims=True), own)
    weights = jnp.exp(scores - peak)
    own_weight = jnp.exp(own - peak)
    total = jnp.sum(weights, axis=1, keepdims=True) + own_weight
    probs = (weights / total).astype(BF)
    own_prob = (own_weight / total).astype(BF).astype(F32)
    result = dot(probs, cv[...]) + own_prob * nv_ref[...].astype(F32)
    result = result.astype(BF)
    for h in range(6):
        att_ref[:, h * 128 : (h + 1) * 128] = result[h : h + 1, :]


def kernel(
    q_hbm, ck_hbm, cv_hbm, nk_hbm, nv_hbm, len_hbm, x_hbm, rw_hbm, ids_hbm, gate_hbm, up_hbm, down_hbm,
    att_ref, out_ref,
    q_ref, nk_ref, nv_ref, len_ref, x_ref, rw_ref, ids_ref, ck, cv, wg, wu, wd, pk, ra, ga, lhs, accg, accu, hid, sb, rb, pe, rc, lp, lr,
    small_sem, loc_sem, wsend, wrecv, asend, arecv, gsend, grecv, rsend, rrecv, esend, erecv, lsend, lrecv,
):
    x = lax.axis_index("attn")
    t = lax.axis_index("tp")
    z = lax.axis_index("exp")
    y = t // 2
    c = t % 2
    half = z % 2
    zi = z // 2
    same = half == c

    def dev(xx, tt, zz):
        return (xx, tt, zz)

    def start(src, dst, ssem, rsem, device):
        pltpu.make_async_remote_copy(
            src_ref=src, dst_ref=dst, send_sem=ssem, recv_sem=rsem, device_id=device, device_id_type=MESH
        ).start()

    small = [
        pltpu.make_async_copy(src, dst, small_sem.at[i])
        for i, (src, dst) in enumerate([
            (ids_hbm, ids_ref), (x_hbm, x_ref), (rw_hbm, rw_ref), (q_hbm, q_ref),
            (nk_hbm, nk_ref), (nv_hbm, nv_ref), (len_hbm, len_ref),
        ])
    ]
    for copy in small:
        copy.start()
    locals_ = [
        pltpu.make_async_copy(ck_hbm.at[0], ck, loc_sem.at[0]),
        pltpu.make_async_copy(cv_hbm.at[0], cv, loc_sem.at[1]),
        pltpu.make_async_copy(gate_hbm.at[0], wg.at[0], loc_sem.at[2]),
        pltpu.make_async_copy(up_hbm.at[0], wu.at[0], loc_sem.at[3]),
        pltpu.make_async_copy(down_hbm.at[0], wd.at[pl.ds(0, HID)], loc_sem.at[4]),
    ]

    barrier = pltpu.get_barrier_semaphore()

    def greet(device):
        pl.semaphore_signal(barrier, inc=1, device_id=device, device_id_type=MESH)

    for d in range(8):
        zs = 2 * ((zi + d) % 8) + c
        greet(dev(x, 2 * y + 1 - c, zs))
        if d:
            greet(dev(x, t, zs))
    @pl.when(jnp.logical_not(same))
    def _():
        greet(dev(x, t, 2 * zi + c))

    for dt in range(1, NT):
        greet(dev(x, (t + dt) % NT, z))
    for dy in range(4):
        for dx in range(4):
            if dx or dy:
                greet(dev((x + dx) % 4, 2 * ((y + dy) % 4) + c, z))

    for copy in locals_:
        copy.start()

    small[0].wait()
    ids = ids_ref[...]
    row = [ids[0:1, :], ids[1:2, :]]
    eye = iota((16, 16), 0) == iota((16, 16), 1)
    col = [jnp.sum(jnp.where(eye, r, 0), axis=1, keepdims=True) for r in row]
    low = iota((16, 16), 0) < iota((16, 16), 1)
    high = iota((16, 16), 1) < iota((16, 16), 0)

    def count(mask, axis):
        return jnp.sum(mask.astype(jnp.int32), axis=axis, keepdims=True)

    same00, same11 = col[0] == row[0], col[1] == row[1]
    slot_row = [
        count(same00 & low, 0),
        count(col[0] == row[1], 0) + count(same11 & low, 0),
    ]
    slot_col = [
        count(same00 & high, 1),
        count(col[1] == row[0], 1) + count(same11 & high, 1),
    ]

    place = iota((128, 16), 0)
    expert, m = place >> 4, place & 15
    chunk = chunk_of(m)
    slot = m - 5 * chunk
    taken = ((row[0] == expert) & (slot_row[0] == slot)) | ((row[1] == expert) & (slot_row[1] == slot))
    packed = jnp.zeros((128, 128), F32)
    small[1].wait()
    for k in range(3):
        mat = jnp.where(taken & (chunk == k), 1.0, 0.0).astype(BF)
        packed = packed + dot(mat, x_ref[:, k * 128 : (k + 1) * 128])
    pk[...] = packed.astype(BF).reshape(8, 16, 128)

    small[2].wait()
    logits = lax.dot_general(x_ref[...], rw_ref[...], (((1,), (1,)), ((), ())), preferred_element_type=F32)
    lp[...] = jnp.zeros((16, 128), F32)
    lp[:, 0:8] = logits

    pl.semaphore_wait(barrier, 15 + 7 + 15 + jnp.where(same, 0, 1))

    mine = 2 * zi + c
    for i in range(1, NZ):
        dz = (i + 1) // 2 if i % 2 else NZ - i // 2
        zt = (z + dz) % NZ
        start(pk.at[zt // 2], ra.at[mine], asend.at[0], arecv, dev(x, 2 * y + half, zt))

    @pl.when(same)
    def _():
        pltpu.make_async_copy(pk.at[zi], ra.at[mine], arecv).start()

    @pl.when(jnp.logical_not(same))
    def _():
        start(pk.at[zi], ra.at[mine], asend.at[1], arecv, dev(x, 2 * y + half, z))

    for dt in range(1, NT):
        start(lp, lr.at[dt - 1], lsend, lrecv, dev(x, (t + dt) % NT, z))

    sibling = dev(x, 2 * y + 1 - c, z)
    start(gate_hbm.at[0], wg.at[1], wsend.at[0], wrecv.at[0], sibling)
    start(up_hbm.at[0], wu.at[1], wsend.at[1], wrecv.at[1], sibling)
    start(down_hbm.at[0], wd.at[pl.ds(HID, HID)], wsend.at[2], wrecv.at[2], sibling)

    for copy in small[3:]:
        copy.wait()
    locals_[0].wait()
    locals_[1].wait()
    attention(q_ref, ck, cv, nk_ref, nv_ref, len_ref, att_ref)

    drain(ra, arecv)
    pick = iota((SLOTROWS, 256), 1)
    pm = pick & 15
    pc = chunk_of(pm)
    spot = ((pick >> 4) & 1) * 40 + (pick >> 5) * 5 + pm - 5 * pc
    here = spot == iota((SLOTROWS, 256), 0)
    arrived = ra[...].reshape(256, 128)
    for k in range(3):
        mat = jnp.where(here & (pc == k), 1.0, 0.0).astype(BF)
        ga[0, 0, :, k * 128 : (k + 1) * 128] = dot(mat, arrived).astype(BF)
    order = [(dx, dy) for dy in range(4) for dx in range(4) if dx or dy]
    for dx, dy in order:
        start(ga.at[0, 0], ga.at[dy, dx], gsend, grecv.at[dy], dev((x + dx) % 4, 2 * ((y + dy) % 4) + c, z))

    locals_[2].wait()
    locals_[3].wait()
    drain(wg.at[1], wrecv.at[0])
    drain(wu.at[1], wrecv.at[1])

    for dy in (0, 1, 3, 2):
        if dy == 0:
            drain(ga.at[0, pl.ds(1, 3)], grecv.at[0])
        else:
            drain(ga.at[dy], grecv.at[dy])
        for dx in range(4):
            for k in range(2):
                lhs[dx * 40 : (dx + 1) * 40, k * W : (k + 1) * W] = ga[dy, dx, k * 40 : (k + 1) * 40, :]
        rows = pl.ds(pl.multiple_of(((y + 4 - dy) % 4) * 768, 768), 768)
        a = lhs[...]
        for h in range(2):
            cols = slice(h * HID, (h + 1) * HID)
            g = dot(a, wg[h, rows, :])
            u = dot(a, wu[h, rows, :])
            if dy:
                g = g + accg[:, cols]
                u = u + accu[:, cols]
            if dy == 2:
                hid[:, cols] = (g / (1.0 + jnp.exp(-g)) * u).astype(BF)
            else:
                accg[:, cols] = g
                accu[:, cols] = u

    locals_[4].wait()
    drain(wd.at[pl.ds(HID, HID)], wrecv.at[2])
    for dy in (2, 1, 3, 0):
        yt = (y + dy) % 4
        term = dot(hid[...], wd[:, pl.ds(pl.multiple_of(yt * 768, 768), 768)]).astype(BF)
        for dx in range(4):
            block = (4 - dx) % 4
            to = rb if dx == 0 and dy == 0 else sb
            for k in range(2):
                to[dy, dx, k * 40 : (k + 1) * 40, :] = term[block * 40 : (block + 1) * 40, k * W : (k + 1) * W]
            if dx or dy:
                start(sb.at[dy, dx], rb.at[dy, dx], rsend, rrecv.at[dy], dev((x + dx) % 4, 2 * yt + c, z))

    total = rb[0, 0].astype(F32)
    for dy in (0, 1, 3, 2):
        if dy == 0:
            drain(rb.at[0, pl.ds(1, 3)], rrecv.at[0])
        else:
            drain(rb.at[dy], rrecv.at[dy])
        for dx in range(4):
            if dx or dy:
                total = total + rb[dy, dx].astype(F32)
    summed = total.astype(BF)

    place = iota((256, SLOTROWS), 0)
    m = place & 15
    chunk = chunk_of(m)
    spot = ((place >> 4) & 1) * 40 + (place >> 5) * 5 + m - 5 * chunk
    here = spot == iota((256, SLOTROWS), 1)
    back = jnp.zeros((256, 128), F32)
    for k in range(3):
        mat = jnp.where(here & (chunk == k), 1.0, 0.0).astype(BF)
        back = back + dot(mat, summed[:, k * 128 : (k + 1) * 128])
    pe[...] = back.astype(BF).reshape(16, 16, 128)
    for d in (4, 3, 5, 2, 6, 1, 7, 0):
        zt = (zi + d) % 8
        for b in range(2):
            ct = (c + b) % 2
            if d or b:
                start(pe.at[2 * zt + ct], rc.at[z], esend.at[0], erecv, dev(x, 2 * y + ct, 2 * zt + c))

    @pl.when(same)
    def _():
        pltpu.make_async_copy(pe.at[2 * zi + c], rc.at[z], erecv).start()

    @pl.when(jnp.logical_not(same))
    def _():
        start(pe.at[2 * zi + c], rc.at[z], esend.at[1], erecv, dev(x, t, 2 * zi + c))

    drain(lr, lrecv)
    full = lp[...]
    for dt in range(NT - 1):
        full = full + lr[dt]
    lane = iota((16, 128), 1)
    chosen = [jnp.sum(jnp.where(lane == col[k], full, 0.0), axis=1, keepdims=True) for k in range(2)]
    mixing = [1.0 / (1.0 + jnp.exp(chosen[1 - k] - chosen[k])) for k in range(2)]

    place = iota((16, 256), 1)
    m = place & 15
    chunk = chunk_of(m)
    slot = m - 5 * chunk
    own = [(col[k] == (place >> 5)) & (slot_col[k] == slot) for k in range(2)]
    drain(rc, erecv)
    returned = rc[...].reshape(256, 128)
    for k in range(3):
        value = [
            dot(jnp.where(own[j] & (chunk == k), 1.0, 0.0).astype(BF), returned) for j in range(2)
        ]
        out_ref[:, k * 128 : (k + 1) * 128] = (mixing[0] * value[0] + mixing[1] * value[1]).astype(BF)

    drain(ra.at[pl.ds(0, 15)], asend.at[0])
    drain(rc.at[pl.ds(0, 15)], esend.at[0])

    @pl.when(jnp.logical_not(same))
    def _():
        drain(ra.at[0], asend.at[1])
        drain(rc.at[0], esend.at[1])

    drain(lr, lsend)
    drain(wg.at[1], wsend.at[0])
    drain(wu.at[1], wsend.at[1])
    drain(wd.at[pl.ds(HID, HID)], wsend.at[2])
    for dy in range(4):
        if dy == 0:
            drain(ga.at[0, pl.ds(1, 3)], gsend)
            drain(rb.at[0, pl.ds(1, 3)], rsend)
        else:
            drain(ga.at[dy], gsend)
            drain(rb.at[dy], rsend)


def body(
    queries, cache_keys, cache_values, new_keys, new_values, lengths,
    moe_input, router_weight, expert_ids, gate_weight, up_weight, down_weight,
):
    vm = pl.BlockSpec(memory_space=pltpu.VMEM)
    hbm = pl.BlockSpec(memory_space=pltpu.HBM)
    dma = pltpu.SemaphoreType.DMA
    return pl.pallas_call(
        kernel,
        out_shape=(
            jax.ShapeDtypeStruct((1, 768), BF),
            jax.ShapeDtypeStruct((16, W), BF),
        ),
        in_specs=[hbm] * 12,
        out_specs=(vm, vm),
        scratch_shapes=[
            pltpu.VMEM((1, 768), BF),
            pltpu.VMEM((1, 128), BF),
            pltpu.VMEM((1, 128), BF),
            pltpu.VMEM((1, 1), jnp.int32),
            pltpu.VMEM((16, W), BF),
            pltpu.VMEM((8, W), BF),
            pltpu.VMEM((2, 16), jnp.int32),
            pltpu.VMEM((512, 128), BF),
            pltpu.VMEM((512, 128), BF),
            pltpu.VMEM((2, D, HID), BF),
            pltpu.VMEM((2, D, HID), BF),
            pltpu.VMEM((2 * HID, D), BF),
            pltpu.VMEM((8, 16, 128), BF),
            pltpu.VMEM((16, 16, 128), BF),
            pltpu.VMEM((4, 4, SLOTROWS, W), BF),
            pltpu.VMEM((160, 768), BF),
            pltpu.VMEM((160, 2 * HID), F32),
            pltpu.VMEM((160, 2 * HID), F32),
            pltpu.VMEM((160, 2 * HID), BF),
            pltpu.VMEM((4, 4, SLOTROWS, W), BF),
            pltpu.VMEM((4, 4, SLOTROWS, W), BF),
            pltpu.VMEM((16, 16, 128), BF),
            pltpu.VMEM((16, 16, 128), BF),
            pltpu.VMEM((16, 128), F32),
            pltpu.VMEM((7, 16, 128), F32),
            dma((7,)),
            dma((5,)),
            dma((3,)),
            dma((3,)),
            dma((2,)),
            dma,
            dma,
            dma((4,)),
            dma,
            dma((4,)),
            dma((2,)),
            dma,
            dma,
            dma,
        ],
        compiler_params=pltpu.CompilerParams(
            collective_id=0, has_side_effects=True, vmem_limit_bytes=60 * 1024 * 1024
        ),
        cost_estimate=pl.CostEstimate(flops=1600000000, bytes_accessed=5500000, transcendentals=100000),
    )(
        queries, cache_keys, cache_values, new_keys, new_values, lengths.reshape(1, 1),
        moe_input, router_weight, expert_ids.T, gate_weight, up_weight, down_weight,
    )


def solution(mesh):
    placed = (
        P(("attn", "exp"), "tp"),
        P(("attn", "exp"), None, "tp"),
        P(("attn", "exp"), None, "tp"),
        P(("attn", "exp"), "tp"),
        P(("attn", "exp"), "tp"),
        P(("attn", "exp")),
        P(("attn", "exp"), "tp"),
        P(None, "tp"),
        P(("attn", "exp"), None),
        P("exp", None, ("attn", "tp")),
        P("exp", None, ("attn", "tp")),
        P("exp", ("attn", "tp"), None),
    )
    return jax.shard_map(
        body,
        mesh=mesh,
        in_specs=placed,
        out_specs=(P(("attn", "exp"), "tp"), P(("attn", "exp"), "tp")),
        check_vma=False,
    )
```

time: 465 us -> 66 us (0.14); the launches traced: 459 us -> 65.8 us
  waiting for transfers between devices: 148 us -> 0 us
  matrix products: 129 us -> 0 us
  loops' own time: 85.5 us -> 0 us
  Pallas kernels: 0 us -> 61.9 us
  blocking collectives: 39.4 us -> 0 us
  local copies, waits for them, and re-layouts: 26.2 us -> 2.55 us
  between operations: 15 us -> 1.29 us
  starting transfers between devices: 12.1 us -> 0 us
    dot_general x101 -> x0, matrix products: 129 us -> none  [the longest x32 55.3 us: one_term(): jnp.einsum('pml,plg->pmg', row_tile_block, down_projection_columns, prefe...]
    another operation x2 -> x0, loops' own time: 85.5 us -> none  [the longest x1 83.9 us: body(): lax.map(one_term, jnp.arange(1 * lax.axis_size(('attn', 'tp')), dtype=jnp...]
    reduce_scatter x1 -> x0, waiting for transfers between devices: 82.3 us -> none  [body(): lax.psum_scatter(lax.map(one_term, jnp.arange(1 * lax.axis_size(('attn',...]
    pallas_call x0 -> x1, Pallas kernels: none -> 61.9 us  [body(): pl.pallas_call(kernel, out_shape=(jax.ShapeDtypeStruct((1, 768), BF), jax...]
    all_gather x1 -> x0, waiting for transfers between devices: 54.3 us -> none  [body(): piece = lax.all_gather(arrived[None], ('attn', 'tp'), axis=0, tiled=True)]
    all_to_all x1 -> x0, blocking collectives: 27.4 us -> none  [body(): lax.all_to_all(packed, 'exp', split_axis=0, concat_axis=1, tiled=True)]
    dynamic_slice x32 -> x0, local copies, waits for them, and re-layouts: 18.6 us -> none  [body(): lax.map(one_term, jnp.arange(1 * lax.axis_size(('attn', 'tp')), dtype=jnp...]
    psum x1 -> x0, blocking collectives: 12 us -> none  [body(): logits = lax.psum(partial_logits, 'tp')]
  transfers between devices with their start and end apart: 3 -> 0, of which waited for: 3 -> 0; matrix products, arithmetic and copies ran while one was open for 1% -> 0% of each run, Pallas kernels for 0% -> 0%
where the time goes in v1:
time: 66 us; the launch traced here: 65.8 us
  Pallas kernels  61.9 us (94%)
  local copies, waits for them, and re-layouts  2.55 us (4%)
  between operations  1.29 us (2%)
    pallas_call x1, Pallas kernels, body(): pl.pallas_call(kernel, out_shape=(jax.ShapeDtypeStruct((1, 768), BF), jax...  61.9 us
    unnamed x2, local copies, waits for them, and re-layouts  2.55 us

profile of v1, /device:TPU:1, one launch (start us, length us, event | category | flops | bytes accessed | tf_op | source)
XLA Modules:
  0.0 65.8 jit_solution(9320744413703111647)
XLA Ops:
  1.3 61.9 %shard_map.131 = (bf16[1,768]{1,0:T(2,128)(2,1)}, bf16[16,384]{1,0:T(8,128)(2,1)}) custom-call(bf16[1,768]{1,0:T(2,128)(2,1)} %q_hbm.1, bf16[1,512,128]{2,1,0:T(8,128)(2,1)} %ck_hbm.1, bf16[1,512,128]{2,1,0:T(8,128)(2,1)} %cv_hbm.1, bf16[1,128]{1,0:T(2,128)(2,1)} %nk_hbm.1, bf16[1,128]{1,0:T(2,128)(2,1)} %nv_hbm.1, s32[1,1]{1,0:T(1,128)} %bitcast.2.len_hbm, ...), custom_call_target="tpu_custom_call" | custom-call | flops 1600000000 | bytes 5500000 | tf_op jit(solution)/shard_map/pallas_call | solution.py:330
  63.2 1.2 %copy.17 = bf16[1,768]{1,0:T(2,128)(2,1)} copy(bf16[1,768]{1,0:T(2,128)(2,1)} %get-tuple-element.4) | data formatting | bytes 3072
  64.5 1.3 %copy.18 = bf16[16,384]{1,0:T(8,128)(2,1)} copy(bf16[16,384]{1,0:T(8,128)(2,1)} %get-tuple-element.5) | data formatting | bytes 24576

commit v2 on v1

v2 whole, which is shorter than its diff:
```python
import math

import jax
import jax.numpy as jnp
from jax import lax
from jax.experimental import pallas as pl
from jax.experimental.pallas import tpu as pltpu
from jax.sharding import PartitionSpec as P

MESH = pl.DeviceIdType.MESH
BF = jnp.bfloat16
F32 = jnp.float32
NT = 8
W = 384
NG = 4
GS = 8 // NG
RAW = 32 * GS
NEAR = (0, 1, -1, 2, -2, 3, -3, 4)
PLANE = tuple((dx, dy) for dy in (2, 1, 3, 0) for dx in (2, 1, 3, 0) if dx or dy)
HID = 256
D = 3072


def iota(shape, dim):
    return lax.broadcasted_iota(jnp.int32, shape, dim)


def chunk_of(m):
    return (m >= 5).astype(jnp.int32) + (m >= 10).astype(jnp.int32) + (m >= 15).astype(jnp.int32)


def dot(a, b):
    return jnp.dot(a, b, preferred_element_type=F32)


def drain(ref, sem):
    pltpu.make_async_copy(ref, ref, sem).wait()


def attention(q_ref, ck, cv, nk_ref, nv_ref, len_ref, att_ref):
    scale = 1.0 / math.sqrt(128)
    q = q_ref[...]
    heads = [q[:, h * 128 : (h + 1) * 128] for h in range(6)]
    qh = jnp.concatenate(heads + [jnp.zeros((2, 128), BF)], axis=0)
    scores = lax.dot_general(qh, ck[...], (((1,), (1,)), ((), ())), preferred_element_type=F32) * scale
    own = jnp.sum(qh.astype(F32) * nk_ref[...].astype(F32), axis=1, keepdims=True) * scale
    visible = iota(scores.shape, 1) < len_ref[...]
    scores = jnp.where(visible, scores, -jnp.inf)
    peak = jnp.maximum(jnp.max(scores, axis=1, keepdims=True), own)
    weights = jnp.exp(scores - peak)
    own_weight = jnp.exp(own - peak)
    total = jnp.sum(weights, axis=1, keepdims=True) + own_weight
    probs = (weights / total).astype(BF)
    own_prob = (own_weight / total).astype(BF).astype(F32)
    result = dot(probs, cv[...]) + own_prob * nv_ref[...].astype(F32)
    result = result.astype(BF)
    for h in range(6):
        att_ref[:, h * 128 : (h + 1) * 128] = result[h : h + 1, :]


def kernel(
    q_hbm, ck_hbm, cv_hbm, nk_hbm, nv_hbm, len_hbm, x_hbm, rw_hbm, ids_hbm, gate_hbm, up_hbm, down_hbm,
    att_ref, out_ref,
    q_ref, nk_ref, nv_ref, len_ref, x_ref, rw_ref, ids_ref, ck, cv, wg, wu, wd,
    pk, ga, lhs, hid, sb, rb, pe, rc, lp, lr,
    small_sem, loc_sem, wsend, wrecv, asend, arecv, gsend, grecv, rsend, rrecv, esend, erecv, lsend, lrecv,
):
    x = lax.axis_index("attn")
    t = lax.axis_index("tp")
    z = lax.axis_index("exp")
    y = t // 2
    c = t % 2
    half = z % 2
    zi = z // 2
    same = half == c

    def start(src, dst, ssem, rsem, device):
        pltpu.make_async_remote_copy(
            src_ref=src, dst_ref=dst, send_sem=ssem, recv_sem=rsem, device_id=device, device_id_type=MESH
        ).start()

    barrier = pltpu.get_barrier_semaphore()

    def greet(device):
        pl.semaphore_signal(barrier, inc=1, device_id=device, device_id_type=MESH)

    turn = jnp.where((c == 1) & (half == 0), -1, 1)
    source = [2 * ((zi + turn * NEAR[p] + 8) % 8) + c for p in range(8)]

    for p in reversed(range(8)):
        greet((x, 2 * y + 1 - c, source[p]))
        if p:
            greet((x, t, source[p]))

    @pl.when(jnp.logical_not(same))
    def _():
        greet((x, t, source[0]))

    for dx, dy in PLANE:
        greet(((x + dx) % 4, 2 * ((y + dy) % 4) + c, z))
    for dt in range(1, NT):
        greet((x, (t + dt) % NT, z))

    small = [
        pltpu.make_async_copy(src, dst, small_sem.at[i])
        for i, (src, dst) in enumerate([
            (ids_hbm, ids_ref), (x_hbm, x_ref), (rw_hbm, rw_ref), (q_hbm, q_ref),
            (nk_hbm, nk_ref), (nv_hbm, nv_ref), (len_hbm, len_ref),
        ])
    ]
    large = [
        pltpu.make_async_copy(ck_hbm.at[0], ck, loc_sem.at[0]),
        pltpu.make_async_copy(cv_hbm.at[0], cv, loc_sem.at[1]),
        pltpu.make_async_copy(gate_hbm.at[0], wg.at[0], loc_sem.at[2]),
        pltpu.make_async_copy(up_hbm.at[0], wu.at[0], loc_sem.at[3]),
        pltpu.make_async_copy(down_hbm.at[0], wd.at[pl.ds(0, HID)], loc_sem.at[4]),
    ]
    for copy in small:
        copy.start()
    for copy in large:
        copy.start()

    small[0].wait()
    ids = ids_ref[...]
    row = [ids[0:1, :], ids[1:2, :]]
    eye = iota((16, 16), 0) == iota((16, 16), 1)
    col = [jnp.sum(jnp.where(eye, r, 0), axis=1, keepdims=True) for r in row]
    low = iota((16, 16), 0) < iota((16, 16), 1)
    high = iota((16, 16), 1) < iota((16, 16), 0)

    def count(mask, axis):
        return jnp.sum(mask.astype(jnp.int32), axis=axis, keepdims=True)

    same00, same11 = col[0] == row[0], col[1] == row[1]
    slot_row = [
        count(same00 & low, 0),
        count(col[0] == row[1], 0) + count(same11 & low, 0),
    ]
    slot_col = [
        count(same00 & high, 1),
        count(col[1] == row[0], 1) + count(same11 & high, 1),
    ]

    place = iota((128, 16), 0)
    expert, m = place >> 4, place & 15
    chunk = chunk_of(m)
    slot = m - 5 * chunk
    taken = ((row[0] == expert) & (slot_row[0] == slot)) | ((row[1] == expert) & (slot_row[1] == slot))
    packed = jnp.zeros((128, 128), F32)
    small[1].wait()
    for k in range(3):
        mat = jnp.where(taken & (chunk == k), 1.0, 0.0).astype(BF)
        packed = packed + dot(mat, x_ref[:, k * 128 : (k + 1) * 128])
    pk[...] = packed.astype(BF).reshape(8, 16, 128)

    small[2].wait()
    logits = lax.dot_general(x_ref[...], rw_ref[...], (((1,), (1,)), ((), ())), preferred_element_type=F32)
    lp[...] = jnp.zeros((16, 128), F32)
    lp[:, 0:8] = logits

    pl.semaphore_wait(barrier, 15 + 7 + 15 + jnp.where(same, 0, 1))

    def spot(p):
        return ga.at[p // GS, 0, pl.ds(pl.multiple_of(16 * (2 * (p % GS) + c), 16), 16)]

    for p in reversed(range(8)):
        for b in range(2):
            sign = jnp.where((half == 1) & (b == 0), -1, 1)
            target = (zi - sign * NEAR[p] + 8) % 8
            if p:
                start(pk.at[target], spot(p), asend.at[0], arecv.at[p // GS], (x, 2 * y + half, 2 * target + b))
            else:
                @pl.when(half != b)
                def _(target=target, b=b):
                    start(pk.at[target], spot(0), asend.at[0], arecv.at[0], (x, 2 * y + half, 2 * target + b))

    @pl.when(same)
    def _():
        pltpu.make_async_copy(pk.at[zi], spot(0), arecv.at[0]).start()

    @pl.when(jnp.logical_not(same))
    def _():
        start(pk.at[zi], spot(0), asend.at[1], arecv.at[0], (x, 2 * y + half, z))

    sibling = (x, 2 * y + 1 - c, z)
    start(gate_hbm.at[0], wg.at[1], wsend.at[0], wrecv.at[0], sibling)
    start(up_hbm.at[0], wu.at[1], wsend.at[1], wrecv.at[1], sibling)
    start(down_hbm.at[0], wd.at[pl.ds(HID, HID)], wsend.at[2], wrecv.at[2], sibling)

    for dt in range(1, NT):
        start(lp, lr.at[dt - 1], lsend, lrecv, (x, (t + dt) % NT, z))

    for copy in small[3:]:
        copy.wait()
    large[0].wait()
    large[1].wait()
    attention(q_ref, ck, cv, nk_ref, nv_ref, len_ref, att_ref)

    for g in range(NG):
        drain(ga.at[g, 0], arecv.at[g])
        for dx, dy in PLANE:
            start(
                ga.at[g, 0], ga.at[g, 4 * dy + dx], gsend, grecv.at[g],
                ((x + dx) % 4, 2 * ((y + dy) % 4) + c, z),
            )

    for copy in large[2:]:
        copy.wait()
    drain(wg.at[1], wrecv.at[0])
    drain(wu.at[1], wrecv.at[1])
    drain(wd.at[pl.ds(HID, HID)], wrecv.at[2])

    def piece_row(raw):
        m = raw & 15
        chunk = chunk_of(m)
        inner = (raw >> 5) * 5 + m - 5 * chunk
        return jnp.where(chunk == 3, -1, (((raw >> 4) & 1) * 3 + chunk) * 16 + inner)

    unpack = jnp.where(piece_row(iota((96, RAW), 1)) == iota((96, RAW), 0), 1.0, 0.0).astype(BF)
    repack = jnp.where(piece_row(iota((RAW, 96), 0)) == iota((RAW, 96), 1), 1.0, 0.0).astype(BF)

    def group(g, _):
        drain(ga.at[g, pl.ds(1, 15)], grecv.at[g])
        for dy in range(4):
            raw = jnp.concatenate([ga[g, 4 * dy + dx] for dx in range(4)], axis=1)
            rows = dot(unpack, raw).astype(BF)
            for dx in range(4):
                for k in range(6):
                    lhs[dx * 16 : (dx + 1) * 16, dy * 768 + k * 128 : dy * 768 + (k + 1) * 128] = rows[
                        k * 16 : (k + 1) * 16, dx * 128 : (dx + 1) * 128
                    ]
        for h in range(2):
            gate = jnp.zeros((64, HID), F32)
            up = jnp.zeros((64, HID), F32)
            for dy in range(4):
                a = lhs[:, dy * 768 : (dy + 1) * 768]
                features = pl.ds(pl.multiple_of(((y + 4 - dy) % 4) * 768, 768), 768)
                gate = gate + dot(a, wg[h, features, :])
                up = up + dot(a, wu[h, features, :])
            hid[:, h * HID : (h + 1) * HID] = (gate / (1.0 + jnp.exp(-gate)) * up).astype(BF)
        for dy in (2, 1, 3, 0):
            yt = (y + dy) % 4
            term = dot(hid[...], wd[:, pl.ds(pl.multiple_of(yt * 768, 768), 768)]).astype(BF)
            blocks = [(4 - dx) % 4 for dx in range(4)]
            stacked = jnp.concatenate(
                [
                    jnp.concatenate([term[b * 16 : (b + 1) * 16, k * 128 : (k + 1) * 128] for b in blocks], axis=1)
                    for k in range(6)
                ],
                axis=0,
            )
            back = dot(repack, stacked).astype(BF)
            for dx in range(4):
                sb[g, 4 * dy + dx] = back[:, dx * 128 : (dx + 1) * 128]
            for dx in (2, 1, 3, 0):
                if dx or dy:
                    start(
                        sb.at[g, 4 * dy + dx], rb.at[g, 4 * dy + dx], rsend, rrecv.at[g],
                        ((x + dx) % 4, 2 * yt + c, z),
                    )
        return 0

    lax.fori_loop(0, NG, group, 0)

    for g in range(NG):
        drain(rb.at[g, pl.ds(1, 15)], rrecv.at[g])
        total = sb[g, 0].astype(F32)
        for i in range(1, 16):
            total = total + rb[g, i].astype(F32)
        pe[g] = total.astype(BF)
        for q in range(GS):
            p = g * GS + q
            for b in range(2):
                ct = (c + b) % 2
                message = pe.at[g, pl.ds(pl.multiple_of(16 * (2 * q + ct), 16), 16)]
                if p or b:
                    start(message, rc.at[z], esend.at[0], erecv, (x, 2 * y + ct, source[p]))
                else:
                    @pl.when(same)
                    def _(message=message):
                        pltpu.make_async_copy(message, rc.at[z], erecv).start()

                    @pl.when(jnp.logical_not(same))
                    def _(message=message):
                        start(message, rc.at[z], esend.at[1], erecv, (x, t, source[0]))

    drain(lr, lrecv)
    full = lp[...]
    for dt in range(NT - 1):
        full = full + lr[dt]
    lane = iota((16, 128), 1)
    chosen = [jnp.sum(jnp.where(lane == col[k], full, 0.0), axis=1, keepdims=True) for k in range(2)]
    mixing = [1.0 / (1.0 + jnp.exp(chosen[1 - k] - chosen[k])) for k in range(2)]

    place = iota((16, 256), 1)
    m = place & 15
    chunk = chunk_of(m)
    slot = m - 5 * chunk
    own = [(col[k] == (place >> 5)) & (slot_col[k] == slot) for k in range(2)]
    picks = [[jnp.where(own[j] & (chunk == k), 1.0, 0.0).astype(BF) for j in range(2)] for k in range(3)]
    drain(rc, erecv)
    returned = rc[...].reshape(256, 128)
    for k in range(3):
        value = [dot(picks[k][j], returned) for j in range(2)]
        out_ref[:, k * 128 : (k + 1) * 128] = (mixing[0] * value[0] + mixing[1] * value[1]).astype(BF)

    drain(rc.at[pl.ds(0, 15)], asend.at[0])
    drain(rc.at[pl.ds(0, 15)], esend.at[0])

    @pl.when(jnp.logical_not(same))
    def _():
        drain(rc.at[0], asend.at[1])
        drain(rc.at[0], esend.at[1])

    drain(lr, lsend)
    drain(wg.at[1], wsend.at[0])
    drain(wu.at[1], wsend.at[1])
    drain(wd.at[pl.ds(HID, HID)], wsend.at[2])
    drain(ga.at[:, pl.ds(1, 15)], gsend)
    drain(rb.at[:, pl.ds(1, 15)], rsend)


def body(
    queries, cache_keys, cache_values, new_keys, new_values, lengths,
    moe_input, router_weight, expert_ids, gate_weight, up_weight, down_weight,
):
    vm = pl.BlockSpec(memory_space=pltpu.VMEM)
    hbm = pl.BlockSpec(memory_space=pltpu.HBM)
    dma = pltpu.SemaphoreType.DMA
    return pl.pallas_call(
        kernel,
        out_shape=(
            jax.ShapeDtypeStruct((1, 768), BF),
            jax.ShapeDtypeStruct((16, W), BF),
        ),
        in_specs=[hbm] * 12,
        out_specs=(vm, vm),
        scratch_shapes=[
            pltpu.VMEM((1, 768), BF),
            pltpu.VMEM((1, 128), BF),
            pltpu.VMEM((1, 128), BF),
            pltpu.VMEM((1, 1), jnp.int32),
            pltpu.VMEM((16, W), BF),
            pltpu.VMEM((8, W), BF),
            pltpu.VMEM((2, 16), jnp.int32),
            pltpu.VMEM((512, 128), BF),
            pltpu.VMEM((512, 128), BF),
            pltpu.VMEM((2, D, HID), BF),
            pltpu.VMEM((2, D, HID), BF),
            pltpu.VMEM((2 * HID, D), BF),
            pltpu.VMEM((8, 16, 128), BF),
            pltpu.VMEM((NG, 16, RAW, 128), BF),
            pltpu.VMEM((64, D), BF),
            pltpu.VMEM((64, 2 * HID), BF),
            pltpu.VMEM((NG, 16, RAW, 128), BF),
            pltpu.VMEM((NG, 16, RAW, 128), BF),
            pltpu.VMEM((NG, RAW, 128), BF),
            pltpu.VMEM((16, 16, 128), BF),
            pltpu.VMEM((16, 128), F32),
            pltpu.VMEM((7, 16, 128), F32),
            dma((7,)),
            dma((5,)),
            dma((3,)),
            dma((3,)),
            dma((2,)),
            dma((NG,)),
            dma,
            dma((NG,)),
            dma,
            dma((NG,)),
            dma((2,)),
            dma,
            dma,
            dma,
        ],
        compiler_params=pltpu.CompilerParams(
            collective_id=0, has_side_effects=True, vmem_limit_bytes=60 * 1024 * 1024
        ),
        cost_estimate=pl.CostEstimate(flops=1600000000, bytes_accessed=5500000, transcendentals=100000),
    )(
        queries, cache_keys, cache_values, new_keys, new_values, lengths.reshape(1, 1),
        moe_input, router_weight, expert_ids.T, gate_weight, up_weight, down_weight,
    )


def solution(mesh):
    placed = (
        P(("attn", "exp"), "tp"),
        P(("attn", "exp"), None, "tp"),
        P(("attn", "exp"), None, "tp"),
        P(("attn", "exp"), "tp"),
        P(("attn", "exp"), "tp"),
        P(("attn", "exp")),
        P(("attn", "exp"), "tp"),
        P(None, "tp"),
        P(("attn", "exp"), None),
        P("exp", None, ("attn", "tp")),
        P("exp", None, ("attn", "tp")),
        P("exp", ("attn", "tp"), None),
    )
    return jax.shard_map(
        body,
        mesh=mesh,
        in_specs=placed,
        out_specs=(P(("attn", "exp"), "tp"), P(("attn", "exp"), "tp")),
        check_vma=False,
    )
```

time: 66 us -> 57.5 us (0.87)
  Pallas kernels: 61.9 us -> 53.4 us
    pallas_call x1, Pallas kernels: 61.9 us -> 53.4 us  [body(): pl.pallas_call(kernel, out_shape=(jax.ShapeDtypeStruct((1, 768), BF), jax...]
where the time goes in v2:
time: 57.5 us; the launch traced here: 57.3 us
  Pallas kernels  53.4 us (93%)
  local copies, waits for them, and re-layouts  2.55 us (4%)
  between operations  1.29 us (2%)
    pallas_call x1, Pallas kernels, body(): pl.pallas_call(kernel, out_shape=(jax.ShapeDtypeStruct((1, 768), BF), jax...  53.4 us
    unnamed x2, local copies, waits for them, and re-layouts  2.55 us

profile of v2, /device:TPU:1, one launch (start us, length us, event | category | flops | bytes accessed | tf_op | source)
XLA Modules:
  0.0 57.3 jit_solution(7314389320248010204)
XLA Ops:
  1.3 53.4 %shard_map.131 = (bf16[1,768]{1,0:T(2,128)(2,1)}, bf16[16,384]{1,0:T(8,128)(2,1)}) custom-call(bf16[1,768]{1,0:T(2,128)(2,1)} %q_hbm.1, bf16[1,512,128]{2,1,0:T(8,128)(2,1)} %ck_hbm.1, bf16[1,512,128]{2,1,0:T(8,128)(2,1)} %cv_hbm.1, bf16[1,128]{1,0:T(2,128)(2,1)} %nk_hbm.1, bf16[1,128]{1,0:T(2,128)(2,1)} %nv_hbm.1, s32[1,1]{1,0:T(1,128)} %bitcast.2.len_hbm, ...), custom_call_target="tpu_custom_call" | custom-call | flops 1600000000 | bytes 5500000 | tf_op jit(solution)/shard_map/pallas_call | solution.py:330
  54.7 1.2 %copy.17 = bf16[1,768]{1,0:T(2,128)(2,1)} copy(bf16[1,768]{1,0:T(2,128)(2,1)} %get-tuple-element.4) | data formatting | bytes 3072
  55.9 1.3 %copy.18 = bf16[16,384]{1,0:T(8,128)(2,1)} copy(bf16[16,384]{1,0:T(8,128)(2,1)} %get-tuple-element.5) | data formatting | bytes 24576

commit v3 on v2

--- a/solution.py
+++ b/solution.py
@@ -15,6 +15,12 @@
 NG = 4
 GS = 8 // NG
 RAW = 32 * GS
+BLK = 8 * GS
+STEPS = ((2, 1, 3, 0),)
+SPREAD = (0, 1, 3, 2)
+WORK = (0, 1, 3, 2)
+LATE = (0,)
+BACK = (1, 3, 2, 0)
 NEAR = (0, 1, -1, 2, -2, 3, -3, 4)
 PLANE = tuple((dx, dy) for dy in (2, 1, 3, 0) for dx in (2, 1, 3, 0) if dx or dy)
 HID = 256
@@ -70,7 +76,8 @@
     z = lax.axis_index("exp")
     y = t // 2
     c = t % 2
-    half = z % 2
+    odd = z % 2
+    half = 1 - odd
     zi = z // 2
     same = half == c
 
@@ -84,8 +91,8 @@
     def greet(device):
         pl.semaphore_signal(barrier, inc=1, device_id=device, device_id_type=MESH)
 
-    turn = jnp.where((c == 1) & (half == 0), -1, 1)
-    source = [2 * ((zi + turn * NEAR[p] + 8) % 8) + c for p in range(8)]
+    turn = jnp.where((c == 0) & (odd == 0), -1, 1)
+    source = [2 * ((zi + turn * NEAR[p] + 8) % 8) + 1 - c for p in range(8)]
 
     for p in reversed(range(8)):
         greet((x, 2 * y + 1 - c, source[p]))
@@ -165,12 +172,12 @@
 
     for p in reversed(range(8)):
         for b in range(2):
-            sign = jnp.where((half == 1) & (b == 0), -1, 1)
+            sign = jnp.where((odd == 1) & (b == 0), -1, 1)
             target = (zi - sign * NEAR[p] + 8) % 8
             if p:
                 start(pk.at[target], spot(p), asend.at[0], arecv.at[p // GS], (x, 2 * y + half, 2 * target + b))
             else:
-                @pl.when(half != b)
+                @pl.when(odd != b)
                 def _(target=target, b=b):
                     start(pk.at[target], spot(0), asend.at[0], arecv.at[0], (x, 2 * y + half, 2 * target + b))
 
@@ -196,7 +203,7 @@
     large[1].wait()
     attention(q_ref, ck, cv, nk_ref, nv_ref, len_ref, att_ref)
 
-    for g in range(NG):
+    for g in SPREAD:
         drain(ga.at[g, 0], arecv.at[g])
         for dx, dy in PLANE:
             start(
@@ -214,55 +221,67 @@
         m = raw & 15
         chunk = chunk_of(m)
         inner = (raw >> 5) * 5 + m - 5 * chunk
-        return jnp.where(chunk == 3, -1, (((raw >> 4) & 1) * 3 + chunk) * 16 + inner)
-
-    unpack = jnp.where(piece_row(iota((96, RAW), 1)) == iota((96, RAW), 0), 1.0, 0.0).astype(BF)
-    repack = jnp.where(piece_row(iota((RAW, 96), 0)) == iota((RAW, 96), 1), 1.0, 0.0).astype(BF)
-
-    def group(g, _):
-        drain(ga.at[g, pl.ds(1, 15)], grecv.at[g])
+        return jnp.where(chunk == 3, -1, (((raw >> 4) & 1) * 3 + chunk) * BLK + inner)
+
+    pieces = 6 * BLK
+    unpack = jnp.where(piece_row(iota((pieces, RAW), 1)) == iota((pieces, RAW), 0), 1.0, 0.0).astype(BF)
+    repack = jnp.where(piece_row(iota((RAW, pieces), 0)) == iota((RAW, pieces), 1), 1.0, 0.0).astype(BF)
+
+    def compute(g, send):
         for dy in range(4):
             raw = jnp.concatenate([ga[g, 4 * dy + dx] for dx in range(4)], axis=1)
             rows = dot(unpack, raw).astype(BF)
             for dx in range(4):
                 for k in range(6):
-                    lhs[dx * 16 : (dx + 1) * 16, dy * 768 + k * 128 : dy * 768 + (k + 1) * 128] = rows[
-                        k * 16 : (k + 1) * 16, dx * 128 : (dx + 1) * 128
+                    lhs[dx * BLK : (dx + 1) * BLK, dy * 768 + k * 128 : dy * 768 + (k + 1) * 128] = rows[
+                        k * BLK : (k + 1) * BLK, dx * 128 : (dx + 1) * 128
                     ]
         for h in range(2):
-            gate = jnp.zeros((64, HID), F32)
-            up = jnp.zeros((64, HID), F32)
+            gate = jnp.zeros((4 * BLK, HID), F32)
+            up = jnp.zeros((4 * BLK, HID), F32)
             for dy in range(4):
                 a = lhs[:, dy * 768 : (dy + 1) * 768]
                 features = pl.ds(pl.multiple_of(((y + 4 - dy) % 4) * 768, 768), 768)
                 gate = gate + dot(a, wg[h, features, :])
                 up = up + dot(a, wu[h, features, :])
             hid[:, h * HID : (h + 1) * HID] = (gate / (1.0 + jnp.exp(-gate)) * up).astype(BF)
+        blocks = [(4 - dx) % 4 for dx in range(4)]
+        for step in STEPS:
+            terms = []
+            for dy in step:
+                features = pl.ds(pl.multiple_of(((y + dy) % 4) * 768, 768), 768)
+                terms.append(dot(hid[...], wd[:, features]).astype(BF))
+            for dy, term in zip(step, terms):
+                stacked = jnp.concatenate(
+                    [
+                        jnp.concatenate([term[b * BLK : (b + 1) * BLK, k * 128 : (k + 1) * 128] for b in blocks], axis=1)
+                        for k in range(6)
+                    ],
+                    axis=0,
+                )
+                back = dot(repack, stacked).astype(BF)
+                for dx in range(4):
+                    sb[g, 4 * dy + dx] = back[:, dx * 128 : (dx + 1) * 128]
+            if send:
+                for dy in step:
+                    send_sums(g, dy)
+
+    def send_sums(g, dy):
+        for dx in (2, 1, 3, 0):
+            if dx or dy:
+                start(
+                    sb.at[g, 4 * dy + dx], rb.at[g, 4 * dy + dx], rsend, rrecv.at[g],
+                    ((x + dx) % 4, 2 * ((y + dy) % 4) + c, z),
+                )
+
+    for g in WORK:
+        drain(ga.at[g, pl.ds(1, 15)], grecv.at[g])
+        compute(g, g not in LATE)
+    for g in LATE:
         for dy in (2, 1, 3, 0):
-            yt = (y + dy) % 4
-            term = dot(hid[...], wd[:, pl.ds(pl.multiple_of(yt * 768, 768), 768)]).astype(BF)
-            blocks = [(4 - dx) % 4 for dx in range(4)]
-            stacked = jnp.concatenate(
-                [
-                    jnp.concatenate([term[b * 16 : (b + 1) * 16, k * 128 : (k + 1) * 128] for b in blocks], axis=1)
-                    for k in range(6)
-                ],
-                axis=0,
-            )
-            back = dot(repack, stacked).astype(BF)
-            for dx in range(4):
-                sb[g, 4 * dy + dx] = back[:, dx * 128 : (dx + 1) * 128]
-            for dx in (2, 1, 3, 0):
-                if dx or dy:
-                    start(
-                        sb.at[g, 4 * dy + dx], rb.at[g, 4 * dy + dx], rsend, rrecv.at[g],
-                        ((x + dx) % 4, 2 * yt + c, z),
-                    )
-        return 0
-
-    lax.fori_loop(0, NG, group, 0)
-
-    for g in range(NG):
+            send_sums(g, dy)
+
+    for g in BACK:
         drain(rb.at[g, pl.ds(1, 15)], rrecv.at[g])
         total = sb[g, 0].astype(F32)
         for i in range(1, 16):
@@ -350,8 +369,8 @@
             pltpu.VMEM((2 * HID, D), BF),
             pltpu.VMEM((8, 16, 128), BF),
             pltpu.VMEM((NG, 16, RAW, 128), BF),
-            pltpu.VMEM((64, D), BF),
-            pltpu.VMEM((64, 2 * HID), BF),
+            pltpu.VMEM((4 * BLK, D), BF),
+            pltpu.VMEM((4 * BLK, 2 * HID), BF),
             pltpu.VMEM((NG, 16, RAW, 128), BF),
             pltpu.VMEM((NG, 16, RAW, 128), BF),
             pltpu.VMEM((NG, RAW, 128), BF),

time: 57.5 us -> 54.6 us (0.950)
  Pallas kernels: 53.4 us -> 50.1 us
    pallas_call x1, Pallas kernels: 53.4 us -> 50.1 us  [body(): pl.pallas_call(kernel, out_shape=(jax.ShapeDtypeStruct((1, 768), BF), jax...]
where the time goes in v3:
time: 54.6 us; the launch traced here: 53.9 us
  Pallas kernels  50.1 us (92%)
  local copies, waits for them, and re-layouts  2.55 us (5%)
  between operations  1.29 us (2%)
    pallas_call x1, Pallas kernels, body(): pl.pallas_call(kernel, out_shape=(jax.ShapeDtypeStruct((1, 768), BF), jax...  50.1 us
    unnamed x2, local copies, waits for them, and re-layouts  2.55 us

profile of v3, /device:TPU:1, one launch (start us, length us, event | category | flops | bytes accessed | tf_op | source)
XLA Modules:
  0.0 53.9 jit_solution(5964253454920772066)
XLA Ops:
  1.3 50.1 %shard_map.131 = (bf16[1,768]{1,0:T(2,128)(2,1)}, bf16[16,384]{1,0:T(8,128)(2,1)}) custom-call(bf16[1,768]{1,0:T(2,128)(2,1)} %q_hbm.1, bf16[1,512,128]{2,1,0:T(8,128)(2,1)} %ck_hbm.1, bf16[1,512,128]{2,1,0:T(8,128)(2,1)} %cv_hbm.1, bf16[1,128]{1,0:T(2,128)(2,1)} %nk_hbm.1, bf16[1,128]{1,0:T(2,128)(2,1)} %nv_hbm.1, s32[1,1]{1,0:T(1,128)} %bitcast.2.len_hbm, ...), custom_call_target="tpu_custom_call" | custom-call | flops 1600000000 | bytes 5500000 | tf_op jit(solution)/shard_map/pallas_call | solution.py:349
  51.4 1.2 %copy.17 = bf16[1,768]{1,0:T(2,128)(2,1)} copy(bf16[1,768]{1,0:T(2,128)(2,1)} %get-tuple-element.4) | data formatting | bytes 3072
  52.6 1.3 %copy.18 = bf16[16,384]{1,0:T(8,128)(2,1)} copy(bf16[16,384]{1,0:T(8,128)(2,1)} %get-tuple-element.5) | data formatting | bytes 24576

commit v4 on v3

--- a/solution.py
+++ b/solution.py
@@ -22,7 +22,7 @@
 LATE = (0,)
 BACK = (1, 3, 2, 0)
 NEAR = (0, 1, -1, 2, -2, 3, -3, 4)
-PLANE = tuple((dx, dy) for dy in (2, 1, 3, 0) for dx in (2, 1, 3, 0) if dx or dy)
+PLANE = ((2, 2), (1, 2), (2, 1), (3, 2), (2, 3), (0, 2), (2, 0), (1, 1), (3, 3), (1, 3), (3, 1), (0, 1), (1, 0), (0, 3), (3, 0))
 HID = 256
 D = 3072
 
@@ -263,23 +263,20 @@
                 for dx in range(4):
                     sb[g, 4 * dy + dx] = back[:, dx * 128 : (dx + 1) * 128]
             if send:
-                for dy in step:
-                    send_sums(g, dy)
-
-    def send_sums(g, dy):
-        for dx in (2, 1, 3, 0):
-            if dx or dy:
-                start(
-                    sb.at[g, 4 * dy + dx], rb.at[g, 4 * dy + dx], rsend, rrecv.at[g],
-                    ((x + dx) % 4, 2 * ((y + dy) % 4) + c, z),
-                )
+                send_sums(g)
+
+    def send_sums(g):
+        for dx, dy in PLANE:
+            start(
+                sb.at[g, 4 * dy + dx], rb.at[g, 4 * dy + dx], rsend, rrecv.at[g],
+                ((x + dx) % 4, 2 * ((y + dy) % 4) + c, z),
+            )
 
     for g in WORK:
         drain(ga.at[g, pl.ds(1, 15)], grecv.at[g])
         compute(g, g not in LATE)
     for g in LATE:
-        for dy in (2, 1, 3, 0):
-            send_sums(g, dy)
+        send_sums(g)
 
     for g in BACK:
         drain(rb.at[g, pl.ds(1, 15)], rrecv.at[g])

time: 54.6 us -> 53.9 us (0.987)
  Pallas kernels: 50.1 us -> 49.4 us
    pallas_call x1, Pallas kernels: 50.1 us -> 49.4 us  [body(): pl.pallas_call(kernel, out_shape=(jax.ShapeDtypeStruct((1, 768), BF), jax...]
where the time goes in v4:
time: 53.9 us; the launch traced here: 53.2 us
  Pallas kernels  49.4 us (92%)
  local copies, waits for them, and re-layouts  2.55 us (5%)
  between operations  1.29 us (2%)
    pallas_call x1, Pallas kernels, body(): pl.pallas_call(kernel, out_shape=(jax.ShapeDtypeStruct((1, 768), BF), jax...  49.4 us
    unnamed x2, local copies, waits for them, and re-layouts  2.55 us

profile of v4, /device:TPU:1, one launch (start us, length us, event | category | flops | bytes accessed | tf_op | source)
XLA Modules:
  0.0 53.2 jit_solution(10930497656927065263)
XLA Ops:
  1.3 49.4 %shard_map.131 = (bf16[1,768]{1,0:T(2,128)(2,1)}, bf16[16,384]{1,0:T(8,128)(2,1)}) custom-call(bf16[1,768]{1,0:T(2,128)(2,1)} %q_hbm.1, bf16[1,512,128]{2,1,0:T(8,128)(2,1)} %ck_hbm.1, bf16[1,512,128]{2,1,0:T(8,128)(2,1)} %cv_hbm.1, bf16[1,128]{1,0:T(2,128)(2,1)} %nk_hbm.1, bf16[1,128]{1,0:T(2,128)(2,1)} %nv_hbm.1, s32[1,1]{1,0:T(1,128)} %bitcast.2.len_hbm, ...), custom_call_target="tpu_custom_call" | custom-call | flops 1600000000 | bytes 5500000 | tf_op jit(solution)/shard_map/pallas_call | solution.py:346
  50.6 1.2 %copy.17 = bf16[1,768]{1,0:T(2,128)(2,1)} copy(bf16[1,768]{1,0:T(2,128)(2,1)} %get-tuple-element.4) | data formatting | bytes 3072
  51.9 1.3 %copy.18 = bf16[16,384]{1,0:T(8,128)(2,1)} copy(bf16[16,384]{1,0:T(8,128)(2,1)} %get-tuple-element.5) | data formatting | bytes 24576

commit v5 on v4

--- a/solution.py
+++ b/solution.py
@@ -207,7 +207,7 @@
         drain(ga.at[g, 0], arecv.at[g])
         for dx, dy in PLANE:
             start(
-                ga.at[g, 0], ga.at[g, 4 * dy + dx], gsend, grecv.at[g],
+                ga.at[g, 0], ga.at[g, 4 * dy + dx], gsend, grecv.at[g, dy],
                 ((x + dx) % 4, 2 * ((y + dy) % 4) + c, z),
             )
 
@@ -227,23 +227,43 @@
     unpack = jnp.where(piece_row(iota((pieces, RAW), 1)) == iota((pieces, RAW), 0), 1.0, 0.0).astype(BF)
     repack = jnp.where(piece_row(iota((RAW, pieces), 0)) == iota((RAW, pieces), 1), 1.0, 0.0).astype(BF)
 
+    def arrive(g, dy):
+        drain(ga.at[g, pl.ds(4 * dy, 4) if dy else pl.ds(1, 3)], grecv.at[g, dy])
+
+    def unpack_rows(g, dy):
+        raw = jnp.concatenate([ga[g, 4 * dy + dx] for dx in range(4)], axis=1)
+        rows = dot(unpack, raw).astype(BF)
+        for dx in range(4):
+            for k in range(6):
+                lhs[dx * BLK : (dx + 1) * BLK, dy * 768 + k * 128 : dy * 768 + (k + 1) * 128] = rows[
+                    k * BLK : (k + 1) * BLK, dx * 128 : (dx + 1) * 128
+                ]
+
+    def add_products(sums, dy):
+        a = lhs[:, dy * 768 : (dy + 1) * 768]
+        features = pl.ds(pl.multiple_of(((y + 4 - dy) % 4) * 768, 768), 768)
+        return [
+            sums[2 * h + i] + dot(a, w[h, features, :])
+            for h in range(2)
+            for i, w in enumerate((wg, wu))
+        ]
+
     def compute(g, send):
-        for dy in range(4):
-            raw = jnp.concatenate([ga[g, 4 * dy + dx] for dx in range(4)], axis=1)
-            rows = dot(unpack, raw).astype(BF)
-            for dx in range(4):
-                for k in range(6):
-                    lhs[dx * BLK : (dx + 1) * BLK, dy * 768 + k * 128 : dy * 768 + (k + 1) * 128] = rows[
-                        k * BLK : (k + 1) * BLK, dx * 128 : (dx + 1) * 128
-                    ]
+        sums = [jnp.zeros((4 * BLK, HID), F32)] * 4
+        if g == 3:
+            for dy in (0, 1, 3, 2):
+                arrive(g, dy)
+                unpack_rows(g, dy)
+                sums = add_products(sums, dy)
+        else:
+            for dy in range(4):
+                arrive(g, dy)
+            for dy in range(4):
+                unpack_rows(g, dy)
+            for dy in range(4):
+                sums = add_products(sums, dy)
         for h in range(2):
-            gate = jnp.zeros((4 * BLK, HID), F32)
-            up = jnp.zeros((4 * BLK, HID), F32)
-            for dy in range(4):
-                a = lhs[:, dy * 768 : (dy + 1) * 768]
-                features = pl.ds(pl.multiple_of(((y + 4 - dy) % 4) * 768, 768), 768)
-                gate = gate + dot(a, wg[h, features, :])
-                up = up + dot(a, wu[h, features, :])
+            gate, up = sums[2 * h], sums[2 * h + 1]
             hid[:, h * HID : (h + 1) * HID] = (gate / (1.0 + jnp.exp(-gate)) * up).astype(BF)
         blocks = [(4 - dx) % 4 for dx in range(4)]
         for step in STEPS:
@@ -273,7 +293,6 @@
             )
 
     for g in WORK:
-        drain(ga.at[g, pl.ds(1, 15)], grecv.at[g])
         compute(g, g not in LATE)
     for g in LATE:
         send_sums(g)
@@ -381,7 +400,7 @@
             dma((2,)),
             dma((NG,)),
             dma,
-            dma((NG,)),
+            dma((NG, 4)),
             dma,
             dma((NG,)),
             dma((2,)),

time: 53.9 us -> 54 us (level)
  no operation moved by 1% of the time
where the time goes in v5:
time: 54 us; the launch traced here: 53.3 us
  Pallas kernels  49.5 us (92%)
  local copies, waits for them, and re-layouts  2.55 us (5%)
  between operations  1.29 us (2%)
    pallas_call x1, Pallas kernels, body(): pl.pallas_call(kernel, out_shape=(jax.ShapeDtypeStruct((1, 768), BF), jax...  49.5 us
    unnamed x2, local copies, waits for them, and re-layouts  2.55 us

profile of v5, /device:TPU:1, one launch (start us, length us, event | category | flops | bytes accessed | tf_op | source)
XLA Modules:
  0.0 53.3 jit_solution(8562106723507285953)
XLA Ops:
  1.3 49.5 %shard_map.131 = (bf16[1,768]{1,0:T(2,128)(2,1)}, bf16[16,384]{1,0:T(8,128)(2,1)}) custom-call(bf16[1,768]{1,0:T(2,128)(2,1)} %q_hbm.1, bf16[1,512,128]{2,1,0:T(8,128)(2,1)} %ck_hbm.1, bf16[1,512,128]{2,1,0:T(8,128)(2,1)} %cv_hbm.1, bf16[1,128]{1,0:T(2,128)(2,1)} %nk_hbm.1, bf16[1,128]{1,0:T(2,128)(2,1)} %nv_hbm.1, s32[1,1]{1,0:T(1,128)} %bitcast.2.len_hbm, ...), custom_call_target="tpu_custom_call" | custom-call | flops 1600000000 | bytes 5500000 | tf_op jit(solution)/shard_map/pallas_call | solution.py:365
  50.8 1.2 %copy.17 = bf16[1,768]{1,0:T(2,128)(2,1)} copy(bf16[1,768]{1,0:T(2,128)(2,1)} %get-tuple-element.4) | data formatting | bytes 3072
  52.0 1.3 %copy.18 = bf16[16,384]{1,0:T(8,128)(2,1)} copy(bf16[16,384]{1,0:T(8,128)(2,1)} %get-tuple-element.5) | data formatting | bytes 24576
